TPU v7x, 32 devices: a whole 2x2x4 slice. The times are simulated.
32 devices in a mesh: cells: 8 (over z, y), sub: 4 (over x, core).
Axes of the slice: x: 2, y: 2, z: 4, core: 2. Of those that a mesh axis runs over, the one named last changes fastest.
Arguments:
- leaf_multipoles: bfloat16 [32768, 296], P(('cells', 'sub')), may hold values from -6 to 6
- occupancy: int32 [32768], P(('cells', 'sub')), may hold values 0 or 1
- upward_maps: bfloat16 [2368, 296], replicated, may hold values from -0.125 to 0.125
- transfer_maps: bfloat16 [9472, 296], replicated, may hold values from -0.125 to 0.125
- downward_maps: bfloat16 [296, 2368], replicated, may hold values from -0.375 to 0.375
- sources_seven: int32 [32768, 8], P(('cells', 'sub')), may hold values from 0 to 32767, as said below
- classes_seven: int32 [32768, 8], P(('cells', 'sub')), may hold values from 0 to 31
- sources_six: int32 [4096, 8], P(('cells', 'sub')), may hold values from 0 to 4095, as said below
- classes_six: int32 [4096, 8], P(('cells', 'sub')), may hold values from 0 to 31
- sources_five: int32 [512, 8], P(('cells', 'sub')), may hold values from 0 to 511
- classes_five: int32 [512, 8], P(('cells', 'sub')), may hold values from 0 to 31
- sources_four: int32 [64, 8], P(('cells', 'sub')), may hold values from 0 to 63
- classes_four: int32 [64, 8], P(('cells', 'sub')), may hold values from 0 to 31
Outputs:
- leaf_locals: bfloat16 [32768, 296], P(('cells', 'sub'))
Inputs may be any that keep to these rules, and one draw needn't show every extreme that they name: `sources_seven`: each entry lies within half of 1024 positions of its own cell's index. `sources_six`: each entry lies within half of 128 positions of its own cell's index.
All inputs are finite; a program needn't handle non-finite values. No bound on the sum of `occupancy` on one device may be relied on, other than what follows from the above.
Results may differ from a plain program's by a relative error of at most 0.015.
Values may be sent and summed in bfloat16 or wider, within the bound.
A program may use at most 128 MiB of HBM per device.

v0:
```python
import jax
import jax.numpy as jnp
from jax import lax
from jax.sharding import PartitionSpec as P


def shifted(value, axis, steps):
    count = lax.axis_size(axis)
    first, last = (max(0, -steps), min(count, count - steps))
    return lax.ppermute(value, axis, [(source, source + steps) for source in range(first, last)])


def ascend(children, upward_maps):
    width = children.shape[1]
    merged = children.reshape(-1, 8 * width)
    return jnp.dot(merged, upward_maps, preferred_element_type=jnp.float32).astype(jnp.bfloat16)


def descend(parents, downward_maps):
    width = parents.shape[1]
    spread = jnp.dot(parents, downward_maps, preferred_element_type=jnp.float32)
    return spread.reshape(-1, width)


def translate(table, indices, classes, transfer_maps):
    count = indices.shape[0]
    entries = indices.shape[1]
    width = table.shape[1]
    kinds = transfer_maps.shape[0] // width
    blocked = min(count, 512)
    labels = jnp.arange(kinds, dtype=jnp.int32)

    def one_block(pair):
        index_rows, class_rows = pair
        total = jnp.zeros((blocked, kinds, width), jnp.float32)
        for entry in range(entries):
            picked = jnp.take(table, index_rows[:, entry], axis=0).astype(jnp.float32)
            match = class_rows[:, entry][:, None] == labels[None, :]
            total = total + jnp.where(match[:, :, None], picked[:, None, :], 0.0)
        grouped = total.astype(jnp.bfloat16).reshape(blocked, kinds * width)
        return jnp.dot(grouped, transfer_maps, preferred_element_type=jnp.float32)

    result = lax.map(
        one_block, (indices.reshape(-1, blocked, entries), classes.reshape(-1, blocked, entries))
    )
    return result.reshape(count, width)


def neighbour_rows(multi):
    count = multi.shape[0]
    below = shifted(multi, ("cells", "sub"), 1)
    above = shifted(multi, ("cells", "sub"), -1)
    return (below, above, count)


def near_table(multi, below, above, leading, sources):
    count = multi.shape[0]
    place = lax.axis_index(("cells", "sub"))
    first_row = place * count - leading
    window = jnp.concatenate([below, multi, above], axis=0)
    return (window, sources - first_row)


def body(
    leaf_multipoles,
    occupancy,
    upward_maps,
    transfer_maps,
    downward_maps,
    sources_seven,
    classes_seven,
    sources_six,
    classes_six,
    sources_five,
    classes_five,
    sources_four,
    classes_four,
):
    multi_seven = jnp.where(
        occupancy[:, None] > 0, leaf_multipoles, jnp.zeros_like(leaf_multipoles)
    )
    multi_six = ascend(multi_seven, upward_maps)
    multi_five = ascend(multi_six, upward_maps)
    below_seven, above_seven, lead_seven = neighbour_rows(multi_seven)
    table_seven, index_seven = near_table(
        multi_seven, below_seven, above_seven, lead_seven, sources_seven
    )
    below_six, above_six, lead_six = neighbour_rows(multi_six)
    table_six, index_six = near_table(multi_six, below_six, above_six, lead_six, sources_six)
    multi_four = ascend(multi_five, upward_maps)
    gathered, gathered_four = (
        lax.all_gather(multi_five, ("cells", "sub"), axis=0, tiled=True),
        lax.all_gather(multi_four, ("cells", "sub"), axis=0, tiled=True),
    )
    table_five, index_five = (gathered, sources_five)
    table_four, index_four = (gathered_four, sources_four)
    local_four = translate(table_four, index_four, classes_four, transfer_maps).astype(jnp.bfloat16)
    local_five = (
        descend(local_four, downward_maps)
        + translate(table_five, index_five, classes_five, transfer_maps)
    ).astype(jnp.bfloat16)
    local_six = (
        descend(local_five, downward_maps)
        + translate(table_six, index_six, classes_six, transfer_maps)
    ).astype(jnp.bfloat16)
    local_seven = (
        descend(local_six, downward_maps)
        + translate(table_seven, index_seven, classes_seven, transfer_maps)
    ).astype(jnp.bfloat16)
    return local_seven


def solution(mesh):
    in_specs = (
        P(("cells", "sub"), None),
        P(("cells", "sub")),
        P(),
        P(),
        P(),
        P(("cells", "sub"), None),
        P(("cells", "sub"), None),
        P(("cells", "sub"), None),
        P(("cells", "sub"), None),
        P(("cells", "sub"), None),
        P(("cells", "sub"), None),
        P(("cells", "sub"), None),
        P(("cells", "sub"), None),
    )
    out_specs = P(("cells", "sub"), None)
    return jax.shard_map(body, mesh=mesh, in_specs=in_specs, out_specs=out_specs, check_vma=False)
```

profile of v0, /device:TPU:0, one launch (start us, length us, event | category | flops | bytes accessed | tf_op | source)
XLA Modules:
  0.0 360.9 jit_solution(401898451435940667)
XLA Ops:
  12.7 5.4 %collective-permute-start.2 = (bf16[1024,296]{0,1:T(8,128)(2,1)S(1)}, bf16[1024,296]{0,1:T(8,128)(2,1)}, u32[]{:S(2)}, u32[]{:S(2)}) collective-permute-start(bf16[1024,296]{0,1:T(8,128)(2,1)S(1)} %broadcast_select_fusion), channel_id=1, source_target_pairs={{0,1},{1,2},{2,3},{3,4},{4,5},{5,6},{6,7},{7,8},{8,9},{9,10},{10,1... | collective-permute-start | bytes 1818632 | tf_op jit(solution)/shard_map/ppermute | solution.py:10
  24.0 47.2 %all_gather.7 = bf16[512,296]{1,0:T(8,128)(2,1)} all-gather(bf16[16,296]{1,0:T(8,128)(2,1)S(1)} %convolution_convert_fusion.1), channel_id=1, replica_groups=mesh['cells'=8,'sub'=4] {'cells','sub'}, dimensions={0}, use_global_device_ids=true | all-gather | bytes 312576 | tf_op jit(solution)/shard_map/all_gather | solution.py:92
  108.0 37.1 %all-gather = bf16[32,2,296]{2,1,0:T(2,128)(2,1)S(1)} all-gather(bf16[1,2,296]{2,1,0:T(2,128)(2,1)S(1)} %fusion.8), channel_id=1, replica_groups=mesh['cells'=8,'sub'=4] {'cells','sub'}, dimensions={0}, use_global_device_ids=true | all-gather | bytes 39072 | tf_op jit(solution)/shard_map/all_gather | solution.py:93
  160.8 4.8 %fusion.9 = f32[2,2368]{1,0:T(2,128)S(1)} fusion(bf16[296,2368]{1,0:T(8,128)(2,1)S(1)} %copy-done, bf16[2,9472]{1,0:T(2,128)(2,1)S(1)} %reshape.1272, bf16[9472,296]{0,1:T(8,128)(2,1)} %param.26), kind=kOutput, calls=%fused_computation.93 | convolution fusion | flops 14019152 | bytes 7066112 | tf_op jit(solution)/shard_map/dot_general | solution.py:21
  165.8 4.8 %fusion.7 = f32[16,2368]{1,0:T(8,128)S(1)} fusion(bf16[296,2368]{1,0:T(8,128)(2,1)S(1)} %copy-done, f32[16,296]{1,0:T(8,128)S(1)} %reshape.993, bf16[16,9472]{1,0:T(8,128)(2,1)S(1)} %copy-done.3, bf16[9472,296]{0,1:T(8,128)(2,1)} %param.26), kind=kOutput, calls=%fused_computation.89 | convolution fusion | flops 112157952 | bytes 7482880 | tf_op jit(solution)/shard_map/dot_general | solution.py:21
  181.2 6.0 %add_convert_fusion.1 = bf16[128,32,296]{0,2,1:T(8,128)(2,1)} fusion(f32[128,296]{0,1:T(8,128)S(1)} %get-tuple-element.343, f32[128,296]{0,1:T(8,128)S(1)} %get-tuple-element.344, f32[128,296]{0,1:T(8,128)S(1)} %get-tuple-element.345, f32[128,296]{0,1:T(8,128)S(1)} %get-tuple-element.346, f32[128,296]{0,1:T(8,128)S(1)} %get-tuple-element.347, ...), kind=kLoop, calls=%fused_computation.78 | loop fusion | flops 19398656 | bytes 3670016 | tf_op jit(solution)/shard_map/while/body/eval_jaxpr/convert_element_type | solution.py:40
  187.2 5.6 %fusion.5 = f32[128,2368]{1,0:T(8,128)S(1)} fusion(bf16[296,2368]{1,0:T(8,128)(2,1)S(1)} %copy-done, f32[128,296]{0,1:T(8,128)S(1)} %copy.110, bf16[128,9472]{0,1:T(8,128)(2,1)} %bitcast.176, bf16[9472,296]{0,1:T(8,128)(2,1)} %param.26), kind=kOutput, calls=%fused_computation.85 | convolution fusion | flops 897263616 | bytes 10798080 | tf_op jit(solution)/shard_map/dot_general | solution.py:21
  198.8 155.7 %while.8 = (s32[]{:T(128)}, f32[2,512,296]{1,2,0:T(8,128)}, s32[2,512,8]{1,2,0:T(8,128)S(1)}, s32[2,512,8]{1,2,0:T(8,128)S(1)}, bf16[3072,296]{1,0:T(8,128)(2,1)}, /*index=5*/bf16[9472,296]{0,1:T(8,128)(2,1)}, s32[]{:T(128)}) while((s32[]{:T(128)}, f32[2,512,296]{1,2,0:T(8,128)}, s32[2,512,8]{1,2,0:T(8,128)S(1)}, ...), condition=%wide.region_1.6_spmd.clone.clone, body=%wide.region_0.5_spmd.clone.clone.sunk | while | flops 2951196672 | bytes 64791168 | solution.py:43
  198.9 3.8 %gather_fusion.1 = bf16[512,296]{1,0:T(8,128)(2,1)S(1)} fusion(bf16[3072,296]{1,0:T(8,128)(2,1)} %get-tuple-element.450, s32[1024]{0:T(1024)S(1)} %pad_clamp_fusion.41), kind=kCustom, calls=%fused_computation.30.clone.clone.1 | custom fusion | bytes 608256 | tf_op jit(solution)/shard_map/while/body/eval_jaxpr/jit(_take)/gather | solution.py:37
  202.9 3.8 %gather_fusion.2 = bf16[512,296]{1,0:T(8,128)(2,1)S(1)} fusion(bf16[3072,296]{1,0:T(8,128)(2,1)} %get-tuple-element.450, s32[1024]{0:T(1024)S(1)} %pad_clamp_fusion.42), kind=kCustom, calls=%fused_computation.29.clone.clone.1 | custom fusion | bytes 608256 | tf_op jit(solution)/shard_map/while/body/eval_jaxpr/jit(_take)/gather | solution.py:37
  212.7 4.4 %gather_fusion.4 = bf16[512,296]{1,0:T(8,128)(2,1)} fusion(bf16[3072,296]{1,0:T(8,128)(2,1)} %get-tuple-element.450, s32[1024]{0:T(1024)S(1)} %pad_clamp_fusion.44), kind=kCustom, calls=%fused_computation.27.clone.clone.1 | custom fusion | bytes 608256 | tf_op jit(solution)/shard_map/while/body/eval_jaxpr/jit(_take)/gather | solution.py:37
  220.8 4.4 %gather_fusion.5 = bf16[512,296]{1,0:T(8,128)(2,1)} fusion(bf16[3072,296]{1,0:T(8,128)(2,1)} %get-tuple-element.450, s32[1024]{0:T(1024)S(1)} %pad_clamp_fusion.45), kind=kCustom, calls=%fused_computation.26.clone.clone.1 | custom fusion | bytes 608256 | tf_op jit(solution)/shard_map/while/body/eval_jaxpr/jit(_take)/gather | solution.py:37
  229.0 4.4 %gather_fusion.6 = bf16[512,296]{1,0:T(8,128)(2,1)} fusion(bf16[3072,296]{1,0:T(8,128)(2,1)} %get-tuple-element.450, s32[1024]{0:T(1024)S(1)} %pad_clamp_fusion.46), kind=kCustom, calls=%fused_computation.25.clone.clone.1 | custom fusion | bytes 608256 | tf_op jit(solution)/shard_map/while/body/eval_jaxpr/jit(_take)/gather | solution.py:37
  237.1 4.4 %gather_fusion.7 = bf16[512,296]{1,0:T(8,128)(2,1)} fusion(bf16[3072,296]{1,0:T(8,128)(2,1)} %get-tuple-element.450, s32[1024]{0:T(1024)S(1)} %pad_clamp_fusion.47), kind=kCustom, calls=%fused_computation.3.clone.clone.1 | custom fusion | bytes 608256 | tf_op jit(solution)/shard_map/while/body/eval_jaxpr/jit(_take)/gather | solution.py:37
  245.3 4.4 %gather_fusion = bf16[512,296]{1,0:T(8,128)(2,1)} fusion(bf16[3072,296]{1,0:T(8,128)(2,1)} %get-tuple-element.450, s32[1024]{0:T(1024)S(1)} %pad_clamp_fusion.40), kind=kCustom, calls=%fused_computation.31.clone.clone.1 | custom fusion | bytes 608256 | tf_op jit(solution)/shard_map/while/body/eval_jaxpr/jit(_take)/gather | solution.py:37
  252.9 19.8 %add_convert_fusion.5 = bf16[512,32,296]{0,2,1:T(8,128)(2,1)S(1)} fusion(f32[512,296]{0,1:T(8,128)S(1)} %select_convert_fusion.32, f32[512,296]{0,1:T(8,128)S(1)} %select_convert_fusion.33, f32[512,296]{0,1:T(8,128)S(1)} %select_convert_fusion.34, f32[512,296]{0,1:T(8,128)S(1)} %select_convert_fusion.35, f32[512,296]{0,1:T(8,128)} %select_convert_fusion.36, ...), kind=kLoop, calls=%fused_computation.33.clone.1 | loop fusion | flops 77594624 | bytes 14680064 | tf_op jit(solution)/shard_map/while/body/eval_jaxpr/convert_element_type | solution.py:40
  272.8 3.9 %fusion.46 = f32[2,512,296]{1,2,0:T(8,128)} fusion(f32[2,512,296]{1,2,0:T(8,128)} %get-tuple-element.440, s32[]{:T(128)} %get-tuple-element.439, bf16[512,9472]{0,1:T(8,128)(2,1)S(1)} %bitcast.173, bf16[9472,296]{0,1:T(8,128)(2,1)S(1)} %bitcast.175), kind=kOutput, calls=%fused_computation.35.clone.1 | convolution fusion | flops 2871001088 | bytes 15913472 | tf_op jit(solution)/shard_map/while/body/eval_jaxpr/dot_general | solution.py:41
  290.5 4.4 %gather_fusion.4 = bf16[512,296]{1,0:T(8,128)(2,1)} fusion(bf16[3072,296]{1,0:T(8,128)(2,1)} %get-tuple-element.450, s32[1024]{0:T(1024)S(1)} %pad_clamp_fusion.44), kind=kCustom, calls=%fused_computation.27.clone.clone.1 | custom fusion | bytes 608256 | tf_op jit(solution)/shard_map/while/body/eval_jaxpr/jit(_take)/gather | solution.py:37
  298.6 4.4 %gather_fusion.5 = bf16[512,296]{1,0:T(8,128)(2,1)} fusion(bf16[3072,296]{1,0:T(8,128)(2,1)} %get-tuple-element.450, s32[1024]{0:T(1024)S(1)} %pad_clamp_fusion.45), kind=kCustom, calls=%fused_computation.26.clone.clone.1 | custom fusion | bytes 608256 | tf_op jit(solution)/shard_map/while/body/eval_jaxpr/jit(_take)/gather | solution.py:37
  306.8 4.4 %gather_fusion.6 = bf16[512,296]{1,0:T(8,128)(2,1)} fusion(bf16[3072,296]{1,0:T(8,128)(2,1)} %get-tuple-element.450, s32[1024]{0:T(1024)S(1)} %pad_clamp_fusion.46), kind=kCustom, calls=%fused_computation.25.clone.clone.1 | custom fusion | bytes 608256 | tf_op jit(solution)/shard_map/while/body/eval_jaxpr/jit(_take)/gather | solution.py:37
  315.0 4.4 %gather_fusion.7 = bf16[512,296]{1,0:T(8,128)(2,1)} fusion(bf16[3072,296]{1,0:T(8,128)(2,1)} %get-tuple-element.450, s32[1024]{0:T(1024)S(1)} %pad_clamp_fusion.47), kind=kCustom, calls=%fused_computation.3.clone.clone.1 | custom fusion | bytes 608256 | tf_op jit(solution)/shard_map/while/body/eval_jaxpr/jit(_take)/gather | solution.py:37
  323.1 4.4 %gather_fusion = bf16[512,296]{1,0:T(8,128)(2,1)} fusion(bf16[3072,296]{1,0:T(8,128)(2,1)} %get-tuple-element.450, s32[1024]{0:T(1024)S(1)} %pad_clamp_fusion.40), kind=kCustom, calls=%fused_computation.31.clone.clone.1 | custom fusion | bytes 608256 | tf_op jit(solution)/shard_map/while/body/eval_jaxpr/jit(_take)/gather | solution.py:37
  330.8 19.8 %add_convert_fusion.5 = bf16[512,32,296]{0,2,1:T(8,128)(2,1)S(1)} fusion(f32[512,296]{0,1:T(8,128)S(1)} %select_convert_fusion.32, f32[512,296]{0,1:T(8,128)S(1)} %select_convert_fusion.33, f32[512,296]{0,1:T(8,128)S(1)} %select_convert_fusion.34, f32[512,296]{0,1:T(8,128)S(1)} %select_convert_fusion.35, f32[512,296]{0,1:T(8,128)} %select_convert_fusion.36, ...), kind=kLoop, calls=%fused_computation.33.clone.1 | loop fusion | flops 77594624 | bytes 14680064 | tf_op jit(solution)/shard_map/while/body/eval_jaxpr/convert_element_type | solution.py:40
  350.6 3.9 %fusion.46 = f32[2,512,296]{1,2,0:T(8,128)} fusion(f32[2,512,296]{1,2,0:T(8,128)} %get-tuple-element.440, s32[]{:T(128)} %get-tuple-element.439, bf16[512,9472]{0,1:T(8,128)(2,1)S(1)} %bitcast.173, bf16[9472,296]{0,1:T(8,128)(2,1)S(1)} %bitcast.175), kind=kOutput, calls=%fused_computation.35.clone.1 | convolution fusion | flops 2871001088 | bytes 15913472 | tf_op jit(solution)/shard_map/while/body/eval_jaxpr/dot_general | solution.py:41
  (306 shorter events, 149.8 us)
Async XLA Ops:
  0.0 160.8 %copy-start = (bf16[296,2368]{1,0:T(8,128)(2,1)S(1)}, bf16[296,2368]{1,0:T(8,128)(2,1)}, u32[]{:S(2)}) copy-start(bf16[296,2368]{1,0:T(8,128)(2,1)} %param.27) | copy-start | bytes 4205572
  0.0 22.7 %copy-start.1 = (bf16[2368,296]{0,1:T(8,128)(2,1)S(1)}, bf16[2368,296]{0,1:T(8,128)(2,1)}, u32[]{:S(2)}) copy-start(bf16[2368,296]{0,1:T(8,128)(2,1)} %param.25) | copy-start | bytes 4205572
  0.0 72.0 %copy-start.5 = (s32[2,8]{1,0:T(2,128)S(1)}, s32[2,8]{1,0:T(2,128)}, u32[]{:S(2)}) copy-start(s32[2,8]{1,0:T(2,128)} %param.34) | copy-start | bytes 196
  0.0 77.0 %copy-start.9 = (s32[128,8]{0,1:T(8,128)S(1)}, s32[128,8]{0,1:T(8,128)}, u32[]{:S(2)}) copy-start(s32[128,8]{0,1:T(8,128)} %param.30) | copy-start | bytes 12292
  0.0 80.6 %copy-start.10 = (s32[128,8]{0,1:T(8,128)S(1)}, s32[128,8]{0,1:T(8,128)}, u32[]{:S(2)}) copy-start(s32[128,8]{0,1:T(8,128)} %param.31) | copy-start | bytes 12292
  0.0 81.2 %copy-start.8 = (s32[16,8]{0,1:T(8,128)S(1)}, s32[16,8]{0,1:T(8,128)}, u32[]{:S(2)}) copy-start(s32[16,8]{0,1:T(8,128)} %param.32) | copy-start | bytes 1540
  2.0 104.1 %copy-start.2 = (bf16[1024,296]{0,1:T(8,128)(2,1)}, bf16[1024,296]{0,1:T(8,128)(2,1)S(1)}, u32[]{:S(2)}) copy-start(bf16[1024,296]{0,1:T(8,128)(2,1)S(1)} %broadcast_select_fusion) | copy-start | bytes 1818628
  5.7 148.5 %copy-start.6 = (s32[2,8]{1,0:T(2,128)S(1)}, s32[2,8]{1,0:T(2,128)}, u32[]{:S(2)}) copy-start(s32[2,8]{1,0:T(2,128)} %param.35) | copy-start | bytes 196
  8.4 162.7 %collective-permute-start = (bf16[128,296]{0,1:T(8,128)(2,1)}, bf16[128,296]{0,1:T(8,128)(2,1)}, u32[]{:S(2)}, u32[]{:S(2)}) collective-permute-start(bf16[128,296]{0,1:T(8,128)(2,1)} %convolution_convert_fusion), channel_id=1, source_target_pairs={{0,1},{1,2},{2,3},{3,4},{4,5},{5,6},{6,7},{7,8},{8,9},{9,10},{10,1... | collective-permute-start | bytes 227336 | tf_op jit(solution)/shard_map/ppermute | solution.py:10
  11.4 159.7 %collective-permute-start.1 = (bf16[128,296]{0,1:T(8,128)(2,1)}, bf16[128,296]{0,1:T(8,128)(2,1)}, u32[]{:S(2)}, u32[]{:S(2)}) collective-permute-start(bf16[128,296]{0,1:T(8,128)(2,1)} %convolution_convert_fusion), channel_id=1, source_target_pairs={{1,0},{2,1},{3,2},{4,3},{5,4},{6,5},{7,6},{8,7},{9,8},{10,9},{11,1... | collective-permute-start | bytes 227336 | tf_op jit(solution)/shard_map/ppermute | solution.py:10
  12.7 182.1 %collective-permute-start.2 = (bf16[1024,296]{0,1:T(8,128)(2,1)S(1)}, bf16[1024,296]{0,1:T(8,128)(2,1)}, u32[]{:S(2)}, u32[]{:S(2)}) collective-permute-start(bf16[1024,296]{0,1:T(8,128)(2,1)S(1)} %broadcast_select_fusion), channel_id=1, source_target_pairs={{0,1},{1,2},{2,3},{3,4},{4,5},{5,6},{6,7},{7,8},{8,9},{9,10},{10,1... | collective-permute-start | bytes 1818632 | tf_op jit(solution)/shard_map/ppermute | solution.py:10
  18.1 176.7 %collective-permute-start.3 = (bf16[1024,296]{0,1:T(8,128)(2,1)S(1)}, bf16[1024,296]{0,1:T(8,128)(2,1)}, u32[]{:S(2)}, u32[]{:S(2)}) collective-permute-start(bf16[1024,296]{0,1:T(8,128)(2,1)S(1)} %broadcast_select_fusion), channel_id=1, source_target_pairs={{1,0},{2,1},{3,2},{4,3},{5,4},{6,5},{7,6},{8,7},{9,8},{10,9},{11,1... | collective-permute-start | bytes 1818632 | tf_op jit(solution)/shard_map/ppermute | solution.py:10
  108.0 57.8 %copy-start.3 = (bf16[16,9472]{1,0:T(8,128)(2,1)S(1)}, bf16[16,9472]{1,0:T(8,128)(2,1)}, u32[]{:S(2)}) copy-start(bf16[16,9472]{1,0:T(8,128)(2,1)} %reshape.1273) | copy-start | bytes 909316
  170.9 10.1 %copy-start.17 = (pred[128]{0:T(512)(128)(4,1)S(1)}, pred[128]{0:T(512)(128)(4,1)}, u32[]{:S(2)}) copy-start(pred[128]{0:T(512)(128)(4,1)} %get-tuple-element.209) | copy-start | bytes 388
  170.9 10.1 %copy-start.18 = (pred[128]{0:T(512)(128)(4,1)S(1)}, pred[128]{0:T(512)(128)(4,1)}, u32[]{:S(2)}) copy-start(pred[128]{0:T(512)(128)(4,1)} %get-tuple-element.279) | copy-start | bytes 388
  171.1 9.9 %copy-start.15 = (pred[128]{0:T(512)(128)(4,1)S(1)}, pred[128]{0:T(512)(128)(4,1)}, u32[]{:S(2)}) copy-start(pred[128]{0:T(512)(128)(4,1)} %get-tuple-element.275) | copy-start | bytes 388
  171.1 9.9 %copy-start.16 = (pred[128]{0:T(512)(128)(4,1)S(1)}, pred[128]{0:T(512)(128)(4,1)}, u32[]{:S(2)}) copy-start(pred[128]{0:T(512)(128)(4,1)} %get-tuple-element.277) | copy-start | bytes 388
  172.1 8.9 %copy-start.13 = (pred[128]{0:T(512)(128)(4,1)S(1)}, pred[128]{0:T(512)(128)(4,1)}, u32[]{:S(2)}) copy-start(pred[128]{0:T(512)(128)(4,1)} %get-tuple-element.271) | copy-start | bytes 388
  172.1 8.9 %copy-start.14 = (pred[128]{0:T(512)(128)(4,1)S(1)}, pred[128]{0:T(512)(128)(4,1)}, u32[]{:S(2)}) copy-start(pred[128]{0:T(512)(128)(4,1)} %get-tuple-element.273) | copy-start | bytes 388
  172.4 8.8 %copy-start.11 = (pred[128]{0:T(512)(128)(4,1)S(1)}, pred[128]{0:T(512)(128)(4,1)}, u32[]{:S(2)}) copy-start(pred[128]{0:T(512)(128)(4,1)} %get-tuple-element.267) | copy-start | bytes 388
  251.6 21.2 %slice-start = ((s8[5607424]{0:T(1024)(128)(4,1)}), s8[4194304]{0:T(1024)(128)(4,1)S(1)}, s32[]{:S(2)}) async-start(s8[5607424]{0:T(1024)(128)(4,1)} %bitcast.174), calls=%async_computation | async-start | bytes 8388608 | tf_op jit(solution)/shard_map/while
  252.9 19.8 %slice-start.1 = ((s8[5607424]{0:T(1024)(128)(4,1)}), s8[1413120]{0:T(1024)(128)(4,1)S(1)}, s32[]{:S(2)}) async-start(s8[5607424]{0:T(1024)(128)(4,1)} %bitcast.174), calls=%async_computation.1 | async-start | bytes 2826240 | tf_op jit(solution)/shard_map/while
  329.4 21.2 %slice-start = ((s8[5607424]{0:T(1024)(128)(4,1)}), s8[4194304]{0:T(1024)(128)(4,1)S(1)}, s32[]{:S(2)}) async-start(s8[5607424]{0:T(1024)(128)(4,1)} %bitcast.174), calls=%async_computation | async-start | bytes 8388608 | tf_op jit(solution)/shard_map/while
  330.7 19.8 %slice-start.1 = ((s8[5607424]{0:T(1024)(128)(4,1)}), s8[1413120]{0:T(1024)(128)(4,1)S(1)}, s32[]{:S(2)}) async-start(s8[5607424]{0:T(1024)(128)(4,1)} %bitcast.174), calls=%async_computation.1 | async-start | bytes 2826240 | tf_op jit(solution)/shard_map/while
  (12 other events, 68.6 us)
where the time goes:
time: 364 us; the launch traced here: 361 us
  local copies, waits for them, and re-layouts  138 us (38%)
  other arithmetic  98.4 us (27%)
  blocking collectives  84.3 us (23%)
  matrix products  28.3 us (8%)
  starting transfers between devices  10.9 us (3%)
    gather x64, local copies, waits for them, and re-layouts, one_block(): picked = jnp.take(table, index_rows[:, entry], axis=0).astype(jnp.float32)  116 us
    all_gather x1, blocking collectives, body(): lax.all_gather(multi_five, ('cells', 'sub'), axis=0, tiled=True)  47.2 us
    convert_element_type x5, other arithmetic, one_block(): grouped = total.astype(jnp.bfloat16).reshape(blocked, kinds * width)  47.2 us
    all_gather x1, blocking collectives, body(): lax.all_gather(multi_four, ('cells', 'sub'), axis=0, tiled=True)  37.1 us
    convert_element_type x32, other arithmetic, one_block(): picked = jnp.take(table, index_rows[:, entry], axis=0).astype(jnp.float32)  28.2 us
    dot_general x3, matrix products, descend(): spread = jnp.dot(parents, downward_maps, preferred_element_type=jnp.float32)  15.2 us
    ppermute x4, starting transfers between devices, shifted(): lax.ppermute(value, axis, [(source, source + steps) for source in range(f...  10.9 us
    gather x40, other arithmetic  9.03 us
  transfers between devices with their start and end apart: 4, of which 0 were waited for; matrix products, arithmetic and copies ran while one was open for 25% of the time, Pallas kernels for 0%

commit v1 on v0

v1 whole, which is shorter than its diff:
```python
import functools

import jax
import jax.numpy as jnp
from jax import lax
from jax.experimental import pallas as pl
from jax.experimental.pallas import tpu as pltpu
from jax.sharding import PartitionSpec as P

AXES = ("cells", "sub")
TILE = 256
VMEM_BYTES = 56 * 1024 * 1024


def shifted(value, axis, steps):
    count = lax.axis_size(axis)
    first, last = (max(0, -steps), min(count, count - steps))
    return lax.ppermute(value, axis, [(source, source + steps) for source in range(first, last)])


def ascend(children, upward_maps):
    width = children.shape[1]
    merged = children.reshape(-1, 8 * width)
    return jnp.dot(merged, upward_maps, preferred_element_type=jnp.float32).astype(jnp.bfloat16)


def gather_groups(table, base, index_ref, class_ref, picked, grouped, padded, kinds):
    width = table.shape[0]
    reach = table.shape[1]
    entries = index_ref.shape[0]
    tile = index_ref.shape[1]
    place = lax.broadcasted_iota(jnp.int32, (reach, tile), 0).astype(jnp.int16)
    for j in range(entries):
        index = (index_ref[j : j + 1, :] - base).astype(jnp.int16)
        hot = jnp.where(place == index, jnp.bfloat16(1), jnp.bfloat16(0))
        picked[j] = jnp.dot(table, hot, preferred_element_type=jnp.float32).astype(jnp.bfloat16)
    classes = class_ref[...]
    for j in range(entries - 1, 0, -1):
        total = picked[j].astype(jnp.float32)
        for i in range(j):
            same = classes[i : i + 1, :] == classes[j : j + 1, :]
            total = total + jnp.where(same, picked[i].astype(jnp.float32), 0.0)
        picked[j] = total.astype(jnp.bfloat16)
    small = classes.astype(jnp.int16)

    @pl.loop(0, kinds)
    def _(kind):
        label = kind.astype(jnp.int16)
        value = jnp.zeros((width, tile), jnp.bfloat16)
        for j in range(entries):
            value = jnp.where(small[j : j + 1, :] == label, picked[j], value)
        grouped[pl.ds(pl.multiple_of(kind * padded, 16), width), :] = value


def near_kernel(
    below_ref, own_ref, above_ref, index_ref, class_ref, maps_ref, out_ref, window, picked, grouped, *, kinds
):
    step = pl.program_id(0)
    half = below_ref.shape[0]
    count = own_ref.shape[0]
    tile = index_ref.shape[1]
    padded = grouped.shape[0] // kinds
    reach = tile + 2 * half

    @pl.when(step == 0)
    def _():
        grouped[...] = jnp.zeros_like(grouped)
        window[:, 0:half] = below_ref[...].T
        window[:, half : half + count] = own_ref[...].T
        window[:, half + count :] = above_ref[...].T

    first = pl.multiple_of(step * tile, tile)
    table = window[:, pl.ds(first, reach)]
    gather_groups(table, first, index_ref, class_ref, picked, grouped, padded, kinds)
    far = jnp.dot(maps_ref[...], grouped[...], preferred_element_type=jnp.float32)
    out_ref[...] = far.T


def near_far(below, own, above, index, classes, maps, kinds):
    count, width = own.shape
    half = below.shape[0]
    entries = index.shape[0]
    tile = min(count, TILE)
    total = maps.shape[1]
    whole = lambda shape: pl.BlockSpec(shape, lambda i: (0, 0))
    return pl.pallas_call(
        functools.partial(near_kernel, kinds=kinds),
        grid=(count // tile,),
        in_specs=[
            whole(below.shape),
            whole(own.shape),
            whole(above.shape),
            pl.BlockSpec((entries, tile), lambda i: (0, i)),
            pl.BlockSpec((entries, tile), lambda i: (0, i)),
            whole(maps.shape),
        ],
        out_specs=pl.BlockSpec((tile, width), lambda i: (i, 0)),
        out_shape=jax.ShapeDtypeStruct((count, width), jnp.float32),
        scratch_shapes=[
            pltpu.VMEM((width, count + 2 * half), jnp.bfloat16),
            pltpu.VMEM((entries, width, tile), jnp.bfloat16),
            pltpu.VMEM((total, tile), jnp.bfloat16),
        ],
        compiler_params=pltpu.CompilerParams(vmem_limit_bytes=VMEM_BYTES),
        cost_estimate=pl.CostEstimate(
            flops=2 * count * width * (total + entries * (tile + 2 * half)),
            bytes_accessed=2 * width * total,
            transcendentals=0,
        ),
    )(below, own, above, index, classes, maps)


def far_kernel(
    table_ref, index_ref, class_ref, maps_ref, down_ref, near_ref, out_ref,
    picked, grouped, far, local_five, local_six, local_seven, *, kinds, counts
):
    count_six, count_five, count_four = counts
    padded = grouped.shape[0] // kinds
    grouped[...] = jnp.zeros_like(grouped)
    gather_groups(table_ref[...], 0, index_ref, class_ref, picked, grouped, padded, kinds)
    far[...] = jnp.dot(maps_ref[...], grouped[...], preferred_element_type=jnp.float32).T
    start_four = count_six + count_five

    def descend(parents, local):
        for octant in range(8):
            spread = jnp.dot(parents, down_ref[octant], preferred_element_type=jnp.float32)
            local[:, octant, :] = spread[: local.shape[0]]
        count, _, width = local.shape
        return local[...].reshape(8 * count, width)

    rows_four = far[start_four : start_four + 16, :].astype(jnp.bfloat16)
    five = descend(rows_four, local_five) + far[count_six:start_four, :]
    six = descend(five.astype(jnp.bfloat16), local_six) + far[0:count_six, :]
    seven = descend(six.astype(jnp.bfloat16), local_seven) + near_ref[...]
    out_ref[...] = seven.astype(jnp.bfloat16)


def coarse_far(table, index, classes, maps, down, near, kinds, counts):
    width = table.shape[0]
    entries, tile = index.shape
    total = maps.shape[1]
    return pl.pallas_call(
        functools.partial(far_kernel, kinds=kinds, counts=counts),
        out_shape=jax.ShapeDtypeStruct(near.shape, jnp.bfloat16),
        scratch_shapes=[
            pltpu.VMEM((entries, width, tile), jnp.bfloat16),
            pltpu.VMEM((total, tile), jnp.bfloat16),
            pltpu.VMEM((tile, width), jnp.float32),
            pltpu.VMEM((counts[2], 8, width), jnp.float32),
            pltpu.VMEM((counts[1], 8, width), jnp.float32),
            pltpu.VMEM((counts[0], 8, width), jnp.float32),
        ],
        compiler_params=pltpu.CompilerParams(vmem_limit_bytes=VMEM_BYTES),
        cost_estimate=pl.CostEstimate(
            flops=2 * tile * width * total, bytes_accessed=2 * width * total, transcendentals=0
        ),
    )(table, index, classes, maps, down, near)


def body(
    leaf_multipoles,
    occupancy,
    upward_maps,
    transfer_maps,
    downward_maps,
    sources_seven,
    classes_seven,
    sources_six,
    classes_six,
    sources_five,
    classes_five,
    sources_four,
    classes_four,
):
    width = leaf_multipoles.shape[1]
    kinds = transfer_maps.shape[0] // width
    padded = (width + 15) // 16 * 16
    place = lax.axis_index(AXES)
    count_seven = sources_seven.shape[0]
    count_six = sources_six.shape[0]
    count_five = sources_five.shape[0]
    count_four = sources_four.shape[0]
    half = count_seven // 2

    multi_seven = jnp.where(
        occupancy[:, None] > 0, leaf_multipoles, jnp.zeros_like(leaf_multipoles)
    )
    below = shifted(multi_seven[-half:], AXES, 1)
    above = shifted(multi_seven[:half], AXES, -1)
    multi_six = ascend(multi_seven, upward_maps)
    multi_five = ascend(multi_six, upward_maps)
    table_five = lax.all_gather(multi_five, AXES, axis=0, tiled=True)

    maps = jnp.pad(
        transfer_maps.reshape(kinds, width, width), ((0, 0), (0, padded - width), (0, 0))
    ).reshape(kinds * padded, width).T
    down = downward_maps.reshape(width, 8, width).transpose(1, 0, 2)

    index_seven = (sources_seven - (place * count_seven - half)).T
    near = near_far(below, multi_seven, above, index_seven, classes_seven.T, maps, kinds)

    edges = ascend(jnp.concatenate([below, above], axis=0), upward_maps)
    reach = half // 8
    table_four = ascend(table_five, upward_maps)
    table = jnp.concatenate(
        [edges[:reach], multi_six, edges[reach:], table_five, table_four], axis=0
    )
    start_five = count_six + 2 * reach
    start_four = start_five + table_five.shape[0]
    rest = (-table.shape[0]) % 128
    table = jnp.pad(table, ((0, rest), (0, 0)))
    used = count_six + count_five + count_four
    tile = (used + 16 + 127) // 128 * 128
    index = jnp.concatenate(
        [
            sources_six - (place * count_six - reach),
            sources_five + start_five,
            sources_four + start_four,
        ],
        axis=0,
    )
    index = jnp.pad(index, ((0, tile - used), (0, 0)))
    classes = jnp.concatenate([classes_six, classes_five, classes_four], axis=0)
    classes = jnp.pad(classes, ((0, tile - used), (0, 0)), constant_values=kinds)
    return coarse_far(
        table.T, index.T, classes.T, maps, down, near, kinds, (count_six, count_five, count_four)
    )


def solution(mesh):
    row = P(AXES, None)
    in_specs = (row, P(AXES), P(), P(), P()) + (row,) * 8
    return jax.shard_map(body, mesh=mesh, in_specs=in_specs, out_specs=row, check_vma=False)
```

time: 364 us -> 164 us (0.45)
  other arithmetic: 98.4 us -> 2.88 us
  local copies, waits for them, and re-layouts: 138 us -> 54.7 us
  Pallas kernels: 0 us -> 54.5 us
  blocking collectives: 84.3 us -> 44.3 us
  matrix products: 28.3 us -> 2.13 us
  starting transfers between devices: 10.9 us -> 5.08 us
    gather x64 -> x0, local copies, waits for them, and re-layouts: 116 us -> none  [one_block(): picked = jnp.take(table, index_rows[:, entry], axis=0).astype(jnp.float32)]
    convert_element_type x38 -> x0, other arithmetic: 77.9 us -> none  [the longest x5 47.2 us: one_block(): grouped = total.astype(jnp.bfloat16).reshape(blocked, kinds * width)]
    pallas_call x0 -> x2, Pallas kernels: none -> 54.5 us  [the longest x1 39.5 us: near_far(): pl.pallas_call(functools.partial(near_kernel, kinds=kinds), grid=(count /...]
    all_gather x2 -> x1, blocking collectives: 84.3 us -> 44.3 us  [body(): table_five = lax.all_gather(multi_five, AXES, axis=0, tiled=True)]
    reshape x4, local copies, waits for them, and re-layouts: 2.39 us -> 37.1 us  [the longest x1 17.7 us: body(): transfer_maps.reshape(kinds, width, width)]
    dot_general x5 -> x0, matrix products: 23 us -> none  [the longest x3 15.2 us: descend(): spread = jnp.dot(parents, downward_maps, preferred_element_type=jnp.float32)]
    gather x40 -> x0, other arithmetic: 9.03 us -> none
    pad x0 -> x1, local copies, waits for them, and re-layouts: none -> 6.76 us  [body(): jnp.pad(transfer_maps.reshape(kinds, width, width), ((0, 0), (0, padded -...]
  transfers between devices with their start and end apart: 4 -> 2, of which waited for: 0 -> 0; matrix products, arithmetic and copies ran while one was open for 25% -> 30% of each run, Pallas kernels for 0% -> 0%
where the time goes in v1:
time: 164 us
  local copies, waits for them, and re-layouts  54.7 us (33%)
  Pallas kernels  54.5 us (33%)
  blocking collectives  44.3 us (27%)
  starting transfers between devices  5.08 us (3%)
  other arithmetic  2.88 us (2%)
  matrix products  2.13 us (1%)
    all_gather x1, blocking collectives, body(): table_five = lax.all_gather(multi_five, AXES, axis=0, tiled=True)  44.3 us
    pallas_call x1, Pallas kernels, near_far(): pl.pallas_call(functools.partial(near_kernel, kinds=kinds), grid=(count /...  39.5 us
    reshape x1, local copies, waits for them, and re-layouts, body(): transfer_maps.reshape(kinds, width, width)  17.7 us
    pallas_call x1, Pallas kernels, coarse_far(): pl.pallas_call(functools.partial(far_kernel, kinds=kinds, counts=counts),...  15 us
    reshape x1, local copies, waits for them, and re-layouts, body(): maps = jnp.pad(transfer_maps.reshape(kinds, width, width), ((0, 0), (0, p...  14.1 us
    pad x1, local copies, waits for them, and re-layouts, body(): jnp.pad(transfer_maps.reshape(kinds, width, width), ((0, 0), (0, padded -...  6.76 us
    reshape x2, local copies, waits for them, and re-layouts, body(): down = downward_maps.reshape(width, 8, width).transpose(1, 0, 2)  5.27 us
    ppermute x2, starting transfers between devices, shifted(): lax.ppermute(value, axis, [(source, source + steps) for source in range(f...  5.08 us
  transfers between devices with their start and end apart: 2, of which 0 were waited for; matrix products, arithmetic and copies ran while one was open for 30% of the time, Pallas kernels for 0%

profile of v1, /device:TPU:0, one launch (start us, length us, event | category | flops | bytes accessed | tf_op | source)
XLA Modules:
  0.0 163.8 jit_solution(5050135139851990724)
XLA Ops:
  0.0 1.5 copy.37
  1.5 0.7 broadcast_compare_fusion
  2.5 1.1 fusion
  3.6 1.3 collective-permute-start.1
  4.8 3.8 %collective-permute-start = (bf16[512,296]{1,0:T(8,128)(2,1)}, bf16[512,296]{1,0:T(8,128)(2,1)}, u32[]{:S(2)}, u32[]{:S(2)}) collective-permute-start(bf16[512,296]{1,0:T(8,128)(2,1)} %get-tuple-element.5), channel_id=1, source_target_pairs={{0,1},{1,2},{2,3},{3,4},{4,5},{5,6},{6,7},{7,8},{8,9},{9,10},{10,1... | collective-permute-start | bytes 909320 | tf_op jit(solution)/shard_map/ppermute | solution.py:18
  8.7 0.6 reshape.24
  9.3 0.5 convolution_convert_fusion
  10.5 44.3 %all_gather.3 = bf16[512,296]{1,0:T(8,128)(2,1)S(1)} all-gather(bf16[16,296]{1,0:T(8,128)(2,1)S(1)} %convolution_convert_fusion.3), channel_id=1, replica_groups=mesh['cells'=8,'sub'=4] {'cells','sub'}, dimensions={0}, use_global_device_ids=true | all-gather | bytes 312576 | tf_op jit(solution)/shard_map/all_gather | solution.py:192
  54.8 0.9 copy.39
  56.0 0.6 convolution_convert_fusion.2
  56.9 17.7 %reshape.27 = bf16[32,296,296]{1,0,2:T(8,128)(2,1)} reshape(bf16[9472,296]{0,1:T(8,128)(2,1)} %param.16) | data formatting | bytes 11214848 | tf_op jit(solution)/shard_map/reshape | solution.py:195
  74.6 6.8 %pad.18 = bf16[32,304,296]{1,0,2:T(8,128)(2,1)} pad(bf16[32,296,296]{1,0,2:T(8,128)(2,1)} %reshape.27, bf16[]{:T(256)} %constant.6.clone.1), padding=0_0x0_8x0_0 | pad | bytes 11366402 | tf_op jit(solution)/shard_map/jit(_pad)/pad | solution.py:194
  81.4 14.1 %reshape.28 = bf16[9728,296]{0,1:T(8,128)(2,1)} reshape(bf16[32,304,296]{1,0,2:T(8,128)(2,1)} %pad.18) | data formatting | bytes 11517952 | tf_op jit(solution)/shard_map/reshape | solution.py:196
  95.5 3.8 %reshape.29 = bf16[296,8,296]{2,1,0:T(8,128)(2,1)S(1)} reshape(bf16[296,2368]{1,0:T(8,128)(2,1)} %param.17) | data formatting | bytes 2803712 | tf_op jit(solution)/shard_map/reshape | solution.py:197
  99.4 1.5 copy.46
  101.0 0.6 pad_bitcast_fusion.1
  101.6 0.6 subtract_bitcast_fusion.index_ref
  102.2 1.2 pad_maximum_fusion
  103.4 0.6 reshape.23
  105.0 1.2 concatenate.13
  106.2 0.8 pad_bitcast_fusion.table_ref
  107.0 39.5 %shard_map.127.near_ref = f32[1024,296]{1,0:T(8,128)} custom-call(bf16[512,296]{1,0:T(8,128)(2,1)} %collective-permute-done.below_ref, bf16[1024,296]{1,0:T(8,128)(2,1)} %copy-done.1, bf16[512,296]{1,0:T(8,128)(2,1)} %collective-permute-done.1.above_ref, s32[8,1024]{1,0:T(8,128)} %subtract_bitcast_fusion.index_ref, s32[8,1024]{1,0:T(8,128)} %bitcast.28, ...), custom_call_target="tpu_custom_call" | custom-call | flops 12104761344 | bytes 5758976 | tf_op jit(solution)/shard_map/pallas_call | solution.py:86
  146.6 15.0 %shard_map.128 = bf16[1024,296]{1,0:T(8,128)(2,1)} custom-call(bf16[296,896]{1,0:T(8,128)(2,1)} %pad_bitcast_fusion.table_ref, s32[8,256]{1,0:T(8,128)} %get-tuple-element.10.index_ref, s32[8,256]{1,0:T(8,128)} %get-tuple-element.9.class_ref, bf16[296,9728]{1,0:T(8,128)(2,1)} %bitcast.26, bf16[8,296,296]{2,1,0:T(8,128)(2,1)} %bitcast.27, ...), custom_call_target="tpu_custom_call" | custom-call | flops 1474297856 | bytes 5758976 | tf_op jit(solution)/shard_map/pallas_call | solution.py:142
  161.6 2.2 %copy.44 = bf16[1024,296]{0,1:T(8,128)(2,1)} copy(bf16[1024,296]{1,0:T(8,128)(2,1)} %shard_map.128) | data formatting | bytes 1212416 | tf_op jit(solution)/shard_map/pallas_call | solution.py:142
  (37 shorter events, 2.7 us)
Async XLA Ops:
  0.0 9.3 %copy-start = (bf16[2368,296]{0,1:T(8,128)(2,1)S(1)}, bf16[2368,296]{0,1:T(8,128)(2,1)}, u32[]{:S(2)}) copy-start(bf16[2368,296]{0,1:T(8,128)(2,1)} %param.15) | copy-start | bytes 4205572
  2.5 6.8 %copy-start.1 = (bf16[1024,296]{1,0:T(8,128)(2,1)}, bf16[1024,296]{1,0:T(8,128)(2,1)S(1)}, u32[]{:S(2)}) copy-start(bf16[1024,296]{1,0:T(8,128)(2,1)S(1)} %broadcast_select_fusion.own_ref) | copy-start | bytes 1818628
  3.6 98.7 %collective-permute-start.1 = (bf16[512,296]{1,0:T(8,128)(2,1)}, bf16[512,296]{1,0:T(8,128)(2,1)}, u32[]{:S(2)}, u32[]{:S(2)}) collective-permute-start(bf16[512,296]{1,0:T(8,128)(2,1)} %get-tuple-element.6), channel_id=1, source_target_pairs={{1,0},{2,1},{3,2},{4,3},{5,4},{6,5},{7,6},{8,7},{9,8},{10,9},{11,1... | collective-permute-start | bytes 909320 | tf_op jit(solution)/shard_map/ppermute | solution.py:18
  4.8 97.4 %collective-permute-start = (bf16[512,296]{1,0:T(8,128)(2,1)}, bf16[512,296]{1,0:T(8,128)(2,1)}, u32[]{:S(2)}, u32[]{:S(2)}) collective-permute-start(bf16[512,296]{1,0:T(8,128)(2,1)} %get-tuple-element.5), channel_id=1, source_target_pairs={{0,1},{1,2},{2,3},{3,4},{4,5},{5,6},{6,7},{7,8},{8,9},{9,10},{10,1... | collective-permute-start | bytes 909320 | tf_op jit(solution)/shard_map/ppermute | solution.py:18
  55.7 1.0 copy-start.8
  55.7 1.1 copy-start.9
  55.7 1.2 copy-start.6
  99.3 1.5 copy-start.7
  99.3 1.5 copy-start.4
  99.3 1.5 copy-start.5
  99.3 2.3 %copy-start.3 = (s32[1024,8]{0,1:T(8,128)S(1)}, s32[1024,8]{0,1:T(8,128)}, u32[]{:S(2)}) copy-start(s32[1024,8]{0,1:T(8,128)} %param.18) | copy-start | bytes 98308
  104.0 1.0 copy-start.2

commit v2 on v1

--- a/solution.py
+++ b/solution.py
@@ -24,54 +24,144 @@
     return jnp.dot(merged, upward_maps, preferred_element_type=jnp.float32).astype(jnp.bfloat16)
 
 
-def gather_groups(table, base, index_ref, class_ref, picked, grouped, padded, kinds):
+def gather_groups(table, base, index_ref, class_ref, picked, labels, grouped, kinds):
     width = table.shape[0]
     reach = table.shape[1]
     entries = index_ref.shape[0]
     tile = index_ref.shape[1]
+    height = picked.shape[2]
+    lower = height - width
     place = lax.broadcasted_iota(jnp.int32, (reach, tile), 0).astype(jnp.int16)
+    blank = jnp.zeros((lower, tile), jnp.float32)
+    classes = class_ref[...]
     for j in range(entries):
         index = (index_ref[j : j + 1, :] - base).astype(jnp.int16)
         hot = jnp.where(place == index, jnp.bfloat16(1), jnp.bfloat16(0))
-        picked[j] = jnp.dot(table, hot, preferred_element_type=jnp.float32).astype(jnp.bfloat16)
-    classes = class_ref[...]
+        found = jnp.dot(table, hot, preferred_element_type=jnp.float32)
+        picked[0, j] = jnp.concatenate([found, blank], axis=0).astype(jnp.bfloat16)
+        picked[1, j] = jnp.concatenate([blank, found], axis=0).astype(jnp.bfloat16)
+        wide = jnp.broadcast_to(classes[j : j + 1, :], (16, tile))
+        labels[j] = wide.astype(jnp.int16)
+    none = jnp.zeros((16, tile), jnp.bfloat16)
     for j in range(entries - 1, 0, -1):
-        total = picked[j].astype(jnp.float32)
-        for i in range(j):
-            same = classes[i : i + 1, :] == classes[j : j + 1, :]
-            total = total + jnp.where(same, picked[i].astype(jnp.float32), 0.0)
-        picked[j] = total.astype(jnp.bfloat16)
-    small = classes.astype(jnp.int16)
-
-    @pl.loop(0, kinds)
-    def _(kind):
-        label = kind.astype(jnp.int16)
-        value = jnp.zeros((width, tile), jnp.bfloat16)
+        same = [labels[i] == labels[j] for i in range(j)]
+        for side in range(2):
+            for row in range(0, height, 16):
+                total = picked[side, j, row : row + 16, :]
+                for i in range(j):
+                    total = total + jnp.where(same[i], picked[side, i, row : row + 16, :], none)
+                picked[side, j, row : row + 16, :] = total
+
+    def chosen(side, first, rows, wanted):
+        found = [[none] * len(rows) for _ in wanted]
         for j in range(entries):
-            value = jnp.where(small[j : j + 1, :] == label, picked[j], value)
-        grouped[pl.ds(pl.multiple_of(kind * padded, 16), width), :] = value
+            match = [labels[j] == label for label in wanted]
+            for r, row in enumerate(rows):
+                piece = picked[side, j, row : row + 16, :]
+                for k in range(len(wanted)):
+                    found[k][r] = jnp.where(match[k], piece, found[k][r])
+        return found
+
+    pair = 2 * width
+    span = 96
+    body_rows = height - 16
+
+    @pl.loop(0, kinds // 4)
+    def _(step):
+        kind = step * 4
+        start = pl.multiple_of(step * (2 * pair), 16)
+        wide = [jnp.full((16, tile), kind + k, jnp.int32).astype(jnp.int16) for k in range(4)]
+        for side in range(2):
+            wanted = [wide[side], wide[side + 2]]
+            offset = side * (body_rows + 16)
+            for at in range(0, body_rows, span):
+                rows = list(range(at, min(at + span, body_rows), 16))
+                found = chosen(side, at, [row + 16 * side for row in rows], wanted)
+                for k in range(2):
+                    for r, row in enumerate(rows):
+                        grouped[pl.ds(start + (k * pair + offset + row), 16), :] = found[k][r]
+        low = chosen(0, 0, [body_rows], [wide[0], wide[2]])
+        high = chosen(1, 0, [0], [wide[1], wide[3]])
+        for k in range(2):
+            grouped[pl.ds(start + (k * pair + body_rows), 16), :] = low[k][0] + high[k][0]
+
+
+def spread_kernel(block_ref, out_ref, held, send_sem, recv_sem):
+    groups, members = held.shape[:2]
+    group = lax.axis_index("cells")
+    member = lax.axis_index("sub")
+    near = [(group, lax.rem(member + k, members)) for k in range(1, members)]
+    far = [(lax.rem(group + k, groups), member) for k in range(1, groups)]
+    barrier = pltpu.get_barrier_semaphore()
+    for device in near + far:
+        pl.semaphore_signal(
+            barrier, inc=1, device_id=device, device_id_type=pl.DeviceIdType.MESH
+        )
+    pl.semaphore_wait(barrier, len(near) + len(far))
+    held[group, member] = block_ref[...]
+
+    def exchange(view, devices, first):
+        copies = [
+            pltpu.make_async_remote_copy(
+                src_ref=view,
+                dst_ref=view,
+                send_sem=send_sem.at[first + k],
+                recv_sem=recv_sem.at[first + k],
+                device_id=device,
+                device_id_type=pl.DeviceIdType.MESH,
+            )
+            for k, device in enumerate(devices)
+        ]
+        for copy in copies:
+            copy.start()
+        for copy in copies:
+            copy.wait()
+
+    exchange(held.at[group, member], near, 0)
+    exchange(held.at[group], far, len(near))
+    out_ref[...] = held[...]
+
+
+def spread(block):
+    groups, members = lax.axis_size("cells"), lax.axis_size("sub")
+    count, width = block.shape
+    copies = groups + members - 2
+    shape = (groups, members, count, width)
+    held = pl.pallas_call(
+        spread_kernel,
+        out_shape=jax.ShapeDtypeStruct(shape, block.dtype),
+        in_specs=[pl.BlockSpec(memory_space=pltpu.VMEM)],
+        out_specs=pl.BlockSpec(memory_space=pltpu.VMEM),
+        scratch_shapes=[
+            pltpu.VMEM(shape, block.dtype),
+            pltpu.SemaphoreType.DMA((copies,)),
+            pltpu.SemaphoreType.DMA((copies,)),
+        ],
+        compiler_params=pltpu.CompilerParams(
+            collective_id=0, has_side_effects=True, vmem_limit_bytes=VMEM_BYTES
+        ),
+    )(block)
+    return held.reshape(-1, width)
 
 
 def near_kernel(
-    below_ref, own_ref, above_ref, index_ref, class_ref, maps_ref, out_ref, window, picked, grouped, *, kinds
+    below_ref, own_ref, above_ref, index_ref, class_ref, maps_ref, out_ref, window, picked, labels, grouped, *, kinds
 ):
     step = pl.program_id(0)
     half = below_ref.shape[0]
     count = own_ref.shape[0]
     tile = index_ref.shape[1]
-    padded = grouped.shape[0] // kinds
     reach = tile + 2 * half
 
     @pl.when(step == 0)
     def _():
-        grouped[...] = jnp.zeros_like(grouped)
         window[:, 0:half] = below_ref[...].T
         window[:, half : half + count] = own_ref[...].T
         window[:, half + count :] = above_ref[...].T
 
     first = pl.multiple_of(step * tile, tile)
     table = window[:, pl.ds(first, reach)]
-    gather_groups(table, first, index_ref, class_ref, picked, grouped, padded, kinds)
+    gather_groups(table, first, index_ref, class_ref, picked, labels, grouped, kinds)
     far = jnp.dot(maps_ref[...], grouped[...], preferred_element_type=jnp.float32)
     out_ref[...] = far.T
 
@@ -82,6 +172,7 @@
     entries = index.shape[0]
     tile = min(count, TILE)
     total = maps.shape[1]
+    height = (width + 15) // 16 * 16
     whole = lambda shape: pl.BlockSpec(shape, lambda i: (0, 0))
     return pl.pallas_call(
         functools.partial(near_kernel, kinds=kinds),
@@ -98,7 +189,8 @@
         out_shape=jax.ShapeDtypeStruct((count, width), jnp.float32),
         scratch_shapes=[
             pltpu.VMEM((width, count + 2 * half), jnp.bfloat16),
-            pltpu.VMEM((entries, width, tile), jnp.bfloat16),
+            pltpu.VMEM((2, entries, height, tile), jnp.bfloat16),
+            pltpu.VMEM((entries, 16, tile), jnp.int16),
             pltpu.VMEM((total, tile), jnp.bfloat16),
         ],
         compiler_params=pltpu.CompilerParams(vmem_limit_bytes=VMEM_BYTES),
@@ -112,12 +204,10 @@
 
 def far_kernel(
     table_ref, index_ref, class_ref, maps_ref, down_ref, near_ref, out_ref,
-    picked, grouped, far, local_five, local_six, local_seven, *, kinds, counts
+    picked, labels, grouped, far, local_five, local_six, local_seven, *, kinds, counts
 ):
     count_six, count_five, count_four = counts
-    padded = grouped.shape[0] // kinds
-    grouped[...] = jnp.zeros_like(grouped)
-    gather_groups(table_ref[...], 0, index_ref, class_ref, picked, grouped, padded, kinds)
+    gather_groups(table_ref[...], 0, index_ref, class_ref, picked, labels, grouped, kinds)
     far[...] = jnp.dot(maps_ref[...], grouped[...], preferred_element_type=jnp.float32).T
     start_four = count_six + count_five
 
@@ -139,11 +229,13 @@
     width = table.shape[0]
     entries, tile = index.shape
     total = maps.shape[1]
+    height = (width + 15) // 16 * 16
     return pl.pallas_call(
         functools.partial(far_kernel, kinds=kinds, counts=counts),
         out_shape=jax.ShapeDtypeStruct(near.shape, jnp.bfloat16),
         scratch_shapes=[
-            pltpu.VMEM((entries, width, tile), jnp.bfloat16),
+            pltpu.VMEM((2, entries, height, tile), jnp.bfloat16),
+            pltpu.VMEM((entries, 16, tile), jnp.int16),
             pltpu.VMEM((total, tile), jnp.bfloat16),
             pltpu.VMEM((tile, width), jnp.float32),
             pltpu.VMEM((counts[2], 8, width), jnp.float32),
@@ -174,7 +266,6 @@
 ):
     width = leaf_multipoles.shape[1]
     kinds = transfer_maps.shape[0] // width
-    padded = (width + 15) // 16 * 16
     place = lax.axis_index(AXES)
     count_seven = sources_seven.shape[0]
     count_six = sources_six.shape[0]
@@ -189,11 +280,9 @@
     above = shifted(multi_seven[:half], AXES, -1)
     multi_six = ascend(multi_seven, upward_maps)
     multi_five = ascend(multi_six, upward_maps)
-    table_five = lax.all_gather(multi_five, AXES, axis=0, tiled=True)
-
-    maps = jnp.pad(
-        transfer_maps.reshape(kinds, width, width), ((0, 0), (0, padded - width), (0, 0))
-    ).reshape(kinds * padded, width).T
+    table_five = spread(multi_five)
+
+    maps = transfer_maps.T
     down = downward_maps.reshape(width, 8, width).transpose(1, 0, 2)
 
     index_seven = (sources_seven - (place * count_seven - half)).T

time: 164 us -> 102 us (0.62)
  blocking collectives: 44.3 us -> 0 us
  local copies, waits for them, and re-layouts: 54.7 us -> 17.9 us
  Pallas kernels: 54.5 us -> 73.5 us
    all_gather x1 -> x0, blocking collectives: 44.3 us -> none  [body(): table_five = lax.all_gather(multi_five, AXES, axis=0, tiled=True)]
    reshape x2 -> x1, local copies, waits for them, and re-layouts: 31.8 us -> 1.89 us  [spread(): return held.reshape(-1, width)]
    pallas_call x0 -> x1, Pallas kernels: none -> 20.4 us  [spread(): pl.pallas_call(spread_kernel, out_shape=jax.ShapeDtypeStruct(shape, block...]
    pad x1 -> x0, local copies, waits for them, and re-layouts: 6.76 us -> none  [body(): jnp.pad(transfer_maps.reshape(kinds, width, width), ((0, 0), (0, padded -...]
  transfers between devices with their start and end apart: 2 -> 2, of which waited for: 0 -> 0; matrix products, arithmetic and copies ran while one was open for 30% -> 13% of each run, Pallas kernels for 0% -> 20%
where the time goes in v2:
time: 102 us
  Pallas kernels  73.5 us (72%)
  local copies, waits for them, and re-layouts  17.9 us (18%)
  starting transfers between devices  4.4 us (4%)
  other arithmetic  2.98 us (3%)
  matrix products  2.76 us (3%)
    pallas_call x1, Pallas kernels, near_far(): pl.pallas_call(functools.partial(near_kernel, kinds=kinds), grid=(count /...  38.4 us
    pallas_call x1, Pallas kernels, spread(): pl.pallas_call(spread_kernel, out_shape=jax.ShapeDtypeStruct(shape, block...  20.4 us
    pallas_call x1, Pallas kernels, coarse_far(): pl.pallas_call(functools.partial(far_kernel, kinds=kinds, counts=counts),...  14.7 us
    reshape x2, local copies, waits for them, and re-layouts, body(): down = downward_maps.reshape(width, 8, width).transpose(1, 0, 2)  5.28 us
    ppermute x2, starting transfers between devices, shifted(): lax.ppermute(value, axis, [(source, source + steps) for source in range(f...  4.4 us
    dot_general x4, matrix products, ascend(): jnp.dot(merged, upward_maps, preferred_element_type=jnp.float32)  2.76 us
    pallas_call x1, local copies, waits for them, and re-layouts, coarse_far(): pl.pallas_call(functools.partial(far_kernel, kinds=kinds, counts=counts),...  2.2 us
  transfers between devices with their start and end apart: 2, of which 0 were waited for; matrix products, arithmetic and copies ran while one was open for 13% of the time, Pallas kernels for 20%

profile of v2, /device:TPU:0, one launch (start us, length us, event | category | flops | bytes accessed | tf_op | source)
XLA Modules:
  0.0 101.8 jit_solution(15771372999679221723)
XLA Ops:
  0.0 0.8 broadcast_compare_fusion
  0.8 1.4 %copy.28 = bf16[1024,296]{1,0:T(8,128)(2,1)S(1)} copy(bf16[1024,296]{0,1:T(8,128)(2,1)} %param.13) | data formatting | bytes 1212416 | tf_op args[0]
  2.5 1.0 fusion
  3.5 3.1 %collective-permute-start = (bf16[512,296]{1,0:T(8,128)(2,1)}, bf16[512,296]{1,0:T(8,128)(2,1)}, u32[]{:S(2)}, u32[]{:S(2)}) collective-permute-start(bf16[512,296]{1,0:T(8,128)(2,1)} %get-tuple-element.5), channel_id=1, source_target_pairs={{0,1},{1,2},{2,3},{3,4},{4,5},{5,6},{6,7},{7,8},{8,9},{9,10},{10,1... | collective-permute-start | bytes 909320 | tf_op jit(solution)/shard_map/ppermute | solution.py:18
  6.6 1.3 %collective-permute-start.1 = (bf16[512,296]{1,0:T(8,128)(2,1)}, bf16[512,296]{1,0:T(8,128)(2,1)}, u32[]{:S(2)}, u32[]{:S(2)}) collective-permute-start(bf16[512,296]{1,0:T(8,128)(2,1)} %get-tuple-element.6), channel_id=1, source_target_pairs={{1,0},{2,1},{3,2},{4,3},{5,4},{6,5},{7,6},{8,7},{9,8},{10,9},{11,1... | collective-permute-start | bytes 909320 | tf_op jit(solution)/shard_map/ppermute | solution.py:18
  7.9 0.6 reshape.18
  8.7 0.6 convolution_convert_fusion
  9.5 1.1 %convolution_convert_fusion.3.block_ref = bf16[16,296]{1,0:T(8,128)(2,1)} fusion(bf16[16,2368]{1,0:T(8,128)(2,1)S(1)} %reshape.19, bf16[2368,296]{0,1:T(8,128)(2,1)S(1)} %copy-done), kind=kOutput, calls=%fused_computation.4 | convolution fusion | flops 22434432 | bytes 1487104 | tf_op jit(solution)/shard_map/dot_general | solution.py:24
  10.6 20.4 %shard_map.127 = bf16[8,4,16,296]{3,2,1,0:T(8,128)(2,1)} custom-call(bf16[16,296]{1,0:T(8,128)(2,1)} %convolution_convert_fusion.3.block_ref), custom_call_target="tpu_custom_call" | custom-call | tf_op jit(solution)/shard_map/pallas_call | solution.py:130
  31.0 1.4 %reshape_reshape.3 = bf16[64,2368]{1,0:T(8,128)(2,1)S(1)} reshape(bf16[8,4,16,296]{3,2,1,0:T(8,128)(2,1)} %shard_map.127) | data formatting | bytes 606208 | tf_op jit(solution)/shard_map/reshape;reshape | solution.py:23
  32.4 1.9 %copy.30 = bf16[512,296]{0,1:T(8,128)(2,1)} copy(bf16[512,296]{1,0:T(8,128)(2,1)} %bitcast.27) | data formatting | bytes 606208 | tf_op jit(solution)/shard_map/reshape | solution.py:144
  34.3 0.6 convolution_convert_fusion.2
  35.0 3.8 %reshape.21 = bf16[296,8,296]{2,1,0:T(8,128)(2,1)S(1)} reshape(bf16[296,2368]{1,0:T(8,128)(2,1)} %param.17) | data formatting | bytes 2803712 | tf_op jit(solution)/shard_map/reshape | solution.py:286
  38.8 1.5 %copy.37 = bf16[296,8,296]{2,0,1:T(8,128)(2,1)} copy(bf16[296,8,296]{2,1,0:T(8,128)(2,1)S(1)} %reshape.21) | data formatting | bytes 2803712 | tf_op jit(solution)/shard_map/reshape | solution.py:286
  40.5 0.6 pad_bitcast_fusion.1
  41.1 0.6 subtract_bitcast_fusion.index_ref
  41.7 1.2 %pad_maximum_fusion = bf16[1024,296]{1,0:T(8,128)(2,1)S(1)} fusion(bf16[512,296]{1,0:T(8,128)(2,1)} %collective-permute-done.1.above_ref, bf16[512,296]{1,0:T(8,128)(2,1)} %collective-permute-done.below_ref), kind=kLoop, calls=%fused_computation.5 | loop fusion | flops 1212416 | bytes 1212416 | tf_op jit(solution)/shard_map/concatenate | solution.py:291
  42.9 0.6 reshape.17
  43.5 0.6 convolution_convert_fusion.1
  44.4 1.2 %concatenate.13 = bf16[832,296]{0,1:T(8,128)(2,1)S(1)} concatenate(bf16[64,296]{0,1:T(8,128)(2,1)S(1)} %get-tuple-element.8, bf16[128,296]{0,1:T(8,128)(2,1)S(1)} %convolution_convert_fusion, bf16[64,296]{0,1:T(8,128)(2,1)S(1)} %get-tuple-element.7, bf16[512,296]{0,1:T(8,128)(2,1)S(1)} %copy-done.2, bf16[64,296]{0,1:T(8,128)(2,1)S(1)} %copy.31), dimensions={0} | concatenate | bytes 985088 | tf_op jit(solution)/shard_map/concatenate | solution.py:294
  45.6 0.8 pad_bitcast_fusion.table_ref
  46.5 38.4 %shard_map.128.near_ref = f32[1024,296]{1,0:T(8,128)} custom-call(bf16[512,296]{1,0:T(8,128)(2,1)} %collective-permute-done.below_ref, bf16[1024,296]{1,0:T(8,128)(2,1)} %copy-done.1, bf16[512,296]{1,0:T(8,128)(2,1)} %collective-permute-done.1.above_ref, s32[8,1024]{1,0:T(8,128)} %subtract_bitcast_fusion.index_ref, s32[8,1024]{1,0:T(8,128)} %bitcast.28, ...), custom_call_target="tpu_custom_call" | custom-call | flops 11949572096 | bytes 5607424 | tf_op jit(solution)/shard_map/pallas_call | solution.py:177
  84.9 14.7 %shard_map.129 = bf16[1024,296]{1,0:T(8,128)(2,1)} custom-call(bf16[296,896]{1,0:T(8,128)(2,1)} %pad_bitcast_fusion.table_ref, s32[8,256]{1,0:T(8,128)} %get-tuple-element.10.index_ref, s32[8,256]{1,0:T(8,128)} %get-tuple-element.9.class_ref, bf16[296,9472]{1,0:T(8,128)(2,1)} %bitcast.26, bf16[8,296,296]{2,1,0:T(8,128)(2,1)} %bitcast.24, ...), custom_call_target="tpu_custom_call" | custom-call | flops 1435500544 | bytes 5607424 | tf_op jit(solution)/shard_map/pallas_call | solution.py:233
  99.6 2.2 %copy.35 = bf16[1024,296]{0,1:T(8,128)(2,1)} copy(bf16[1024,296]{1,0:T(8,128)(2,1)} %shard_map.129) | data formatting | bytes 1212416 | tf_op jit(solution)/shard_map/pallas_call | solution.py:233
  (34 shorter events, 1.4 us)
Async XLA Ops:
  0.0 8.7 %copy-start = (bf16[2368,296]{0,1:T(8,128)(2,1)S(1)}, bf16[2368,296]{0,1:T(8,128)(2,1)}, u32[]{:S(2)}) copy-start(bf16[2368,296]{0,1:T(8,128)(2,1)} %param.15) | copy-start | bytes 4205572
  2.5 6.0 %copy-start.1 = (bf16[1024,296]{1,0:T(8,128)(2,1)}, bf16[1024,296]{1,0:T(8,128)(2,1)S(1)}, u32[]{:S(2)}) copy-start(bf16[1024,296]{1,0:T(8,128)(2,1)S(1)} %broadcast_select_fusion.own_ref) | copy-start | bytes 1818628
  2.5 6.1 %copy-start.6 = (s32[16,8]{0,1:T(8,128)S(1)}, s32[16,8]{0,1:T(8,128)}, u32[]{:S(2)}) copy-start(s32[16,8]{0,1:T(8,128)} %param.22) | copy-start | bytes 1540
  2.5 6.1 %copy-start.8 = (s32[2,8]{1,0:T(2,128)S(1)}, s32[2,8]{1,0:T(2,128)}, u32[]{:S(2)}) copy-start(s32[2,8]{1,0:T(2,128)} %param.24) | copy-start | bytes 196
  2.5 6.1 %copy-start.9 = (s32[2,8]{1,0:T(2,128)S(1)}, s32[2,8]{1,0:T(2,128)}, u32[]{:S(2)}) copy-start(s32[2,8]{1,0:T(2,128)} %param.25) | copy-start | bytes 196
  3.5 38.2 %collective-permute-start = (bf16[512,296]{1,0:T(8,128)(2,1)}, bf16[512,296]{1,0:T(8,128)(2,1)}, u32[]{:S(2)}, u32[]{:S(2)}) collective-permute-start(bf16[512,296]{1,0:T(8,128)(2,1)} %get-tuple-element.5), channel_id=1, source_target_pairs={{0,1},{1,2},{2,3},{3,4},{4,5},{5,6},{6,7},{7,8},{8,9},{9,10},{10,1... | collective-permute-start | bytes 909320 | tf_op jit(solution)/shard_map/ppermute | solution.py:18
  6.6 35.1 %collective-permute-start.1 = (bf16[512,296]{1,0:T(8,128)(2,1)}, bf16[512,296]{1,0:T(8,128)(2,1)}, u32[]{:S(2)}, u32[]{:S(2)}) collective-permute-start(bf16[512,296]{1,0:T(8,128)(2,1)} %get-tuple-element.6), channel_id=1, source_target_pairs={{1,0},{2,1},{3,2},{4,3},{5,4},{6,5},{7,6},{8,7},{9,8},{10,9},{11,1... | collective-permute-start | bytes 909320 | tf_op jit(solution)/shard_map/ppermute | solution.py:18
  38.7 1.5 %copy-start.7 = (s32[128,8]{0,1:T(8,128)S(1)}, s32[128,8]{0,1:T(8,128)}, u32[]{:S(2)}) copy-start(s32[128,8]{0,1:T(8,128)} %param.20) | copy-start | bytes 12292
  38.8 1.6 %copy-start.4 = (s32[16,8]{0,1:T(8,128)S(1)}, s32[16,8]{0,1:T(8,128)}, u32[]{:S(2)}) copy-start(s32[16,8]{0,1:T(8,128)} %param.23) | copy-start | bytes 1540
  38.8 1.6 %copy-start.5 = (s32[128,8]{0,1:T(8,128)S(1)}, s32[128,8]{0,1:T(8,128)}, u32[]{:S(2)}) copy-start(s32[128,8]{0,1:T(8,128)} %param.21) | copy-start | bytes 12292
  38.8 2.3 %copy-start.3 = (s32[1024,8]{0,1:T(8,128)S(1)}, s32[1024,8]{0,1:T(8,128)}, u32[]{:S(2)}) copy-start(s32[1024,8]{0,1:T(8,128)} %param.18) | copy-start | bytes 98308
  43.5 1.0 copy-start.2

commit v3 on v2

--- a/solution.py
+++ b/solution.py
@@ -8,7 +8,7 @@
 from jax.sharding import PartitionSpec as P
 
 AXES = ("cells", "sub")
-TILE = 256
+TILE = 512
 VMEM_BYTES = 56 * 1024 * 1024
 
 
@@ -34,12 +34,17 @@
     place = lax.broadcasted_iota(jnp.int32, (reach, tile), 0).astype(jnp.int16)
     blank = jnp.zeros((lower, tile), jnp.float32)
     classes = class_ref[...]
+    for j in range(0, entries, 2):
+        hots = []
+        for i in (j, j + 1):
+            index = (index_ref[i : i + 1, :] - base).astype(jnp.int16)
+            hots.append(jnp.where(place == index, jnp.bfloat16(1), jnp.bfloat16(0)))
+        both = jnp.dot(table, jnp.concatenate(hots, axis=1), preferred_element_type=jnp.float32)
+        for i in (j, j + 1):
+            found = both[:, (i - j) * tile : (i - j + 1) * tile]
+            picked[0, i] = jnp.concatenate([found, blank], axis=0).astype(jnp.bfloat16)
+            picked[1, i] = jnp.concatenate([blank, found], axis=0).astype(jnp.bfloat16)
     for j in range(entries):
-        index = (index_ref[j : j + 1, :] - base).astype(jnp.int16)
-        hot = jnp.where(place == index, jnp.bfloat16(1), jnp.bfloat16(0))
-        found = jnp.dot(table, hot, preferred_element_type=jnp.float32)
-        picked[0, j] = jnp.concatenate([found, blank], axis=0).astype(jnp.bfloat16)
-        picked[1, j] = jnp.concatenate([blank, found], axis=0).astype(jnp.bfloat16)
         wide = jnp.broadcast_to(classes[j : j + 1, :], (16, tile))
         labels[j] = wide.astype(jnp.int16)
     none = jnp.zeros((16, tile), jnp.bfloat16)
@@ -63,7 +68,7 @@
         return found
 
     pair = 2 * width
-    span = 96
+    span = max(16, 96 * 256 // tile // 16 * 16)
     body_rows = height - 16
 
     @pl.loop(0, kinds // 4)
@@ -162,8 +167,7 @@
     first = pl.multiple_of(step * tile, tile)
     table = window[:, pl.ds(first, reach)]
     gather_groups(table, first, index_ref, class_ref, picked, labels, grouped, kinds)
-    far = jnp.dot(maps_ref[...], grouped[...], preferred_element_type=jnp.float32)
-    out_ref[...] = far.T
+    out_ref[...] = jnp.dot(maps_ref[...], grouped[...], preferred_element_type=jnp.float32)
 
 
 def near_far(below, own, above, index, classes, maps, kinds):
@@ -185,8 +189,8 @@
             pl.BlockSpec((entries, tile), lambda i: (0, i)),
             whole(maps.shape),
         ],
-        out_specs=pl.BlockSpec((tile, width), lambda i: (i, 0)),
-        out_shape=jax.ShapeDtypeStruct((count, width), jnp.float32),
+        out_specs=pl.BlockSpec((width, tile), lambda i: (0, i)),
+        out_shape=jax.ShapeDtypeStruct((width, count), jnp.float32),
         scratch_shapes=[
             pltpu.VMEM((width, count + 2 * half), jnp.bfloat16),
             pltpu.VMEM((2, entries, height, tile), jnp.bfloat16),
@@ -212,17 +216,17 @@
     start_four = count_six + count_five
 
     def descend(parents, local):
+        count, _, width = local.shape
+        wide = jnp.dot(parents, down_ref[...], preferred_element_type=jnp.float32)
         for octant in range(8):
-            spread = jnp.dot(parents, down_ref[octant], preferred_element_type=jnp.float32)
-            local[:, octant, :] = spread[: local.shape[0]]
-        count, _, width = local.shape
+            local[:, octant, :] = wide[:count, octant * width : (octant + 1) * width]
         return local[...].reshape(8 * count, width)
 
     rows_four = far[start_four : start_four + 16, :].astype(jnp.bfloat16)
     five = descend(rows_four, local_five) + far[count_six:start_four, :]
     six = descend(five.astype(jnp.bfloat16), local_six) + far[0:count_six, :]
-    seven = descend(six.astype(jnp.bfloat16), local_seven) + near_ref[...]
-    out_ref[...] = seven.astype(jnp.bfloat16)
+    seven = descend(six.astype(jnp.bfloat16), local_seven)
+    out_ref[...] = (seven.T + near_ref[...]).astype(jnp.bfloat16)
 
 
 def coarse_far(table, index, classes, maps, down, near, kinds, counts):
@@ -283,7 +287,6 @@
     table_five = spread(multi_five)
 
     maps = transfer_maps.T
-    down = downward_maps.reshape(width, 8, width).transpose(1, 0, 2)
 
     index_seven = (sources_seven - (place * count_seven - half)).T
     near = near_far(below, multi_seven, above, index_seven, classes_seven.T, maps, kinds)
@@ -312,8 +315,9 @@
     classes = jnp.concatenate([classes_six, classes_five, classes_four], axis=0)
     classes = jnp.pad(classes, ((0, tile - used), (0, 0)), constant_values=kinds)
     return coarse_far(
-        table.T, index.T, classes.T, maps, down, near, kinds, (count_six, count_five, count_four)
-    )
+        table.T, index.T, classes.T, maps, downward_maps, near, kinds,
+        (count_six, count_five, count_four),
+    ).T
 
 
 def solution(mesh):

time: 102 us -> 84.7 us (0.83)
  Pallas kernels: 73.5 us -> 64.3 us
  local copies, waits for them, and re-layouts: 17.9 us -> 9.62 us
    pallas_call x1, Pallas kernels: 38.4 us -> 29.1 us  [near_far(): pl.pallas_call(functools.partial(near_kernel, kinds=kinds), grid=(count /...]
    reshape x2 -> x0, local copies, waits for them, and re-layouts: 5.28 us -> none  [body(): down = downward_maps.reshape(width, 8, width).transpose(1, 0, 2)]
    pallas_call x1 -> x0, local copies, waits for them, and re-layouts: 2.2 us -> none  [coarse_far(): pl.pallas_call(functools.partial(far_kernel, kinds=kinds, counts=counts),...]
  transfers between devices with their start and end apart: 2 -> 2, of which waited for: 0 -> 0; matrix products, arithmetic and copies ran while one was open for 13% -> 9% of each run, Pallas kernels for 20% -> 24%
where the time goes in v3:
time: 84.7 us; the launch traced here: 84.4 us
  Pallas kernels  64.3 us (76%)
  local copies, waits for them, and re-layouts  9.62 us (11%)
  starting transfers between devices  4.39 us (5%)
  other arithmetic  3 us (4%)
  matrix products  2.75 us (3%)
    pallas_call x1, Pallas kernels, near_far(): pl.pallas_call(functools.partial(near_kernel, kinds=kinds), grid=(count /...  29.1 us
    pallas_call x1, Pallas kernels, spread(): pl.pallas_call(spread_kernel, out_shape=jax.ShapeDtypeStruct(shape, block...  20.4 us
    pallas_call x1, Pallas kernels, coarse_far(): pl.pallas_call(functools.partial(far_kernel, kinds=kinds, counts=counts),...  14.8 us
    ppermute x2, starting transfers between devices, shifted(): lax.ppermute(value, axis, [(source, source + steps) for source in range(f...  4.39 us
    dot_general x4, matrix products, ascend(): jnp.dot(merged, upward_maps, preferred_element_type=jnp.float32)  2.75 us
  transfers between devices with their start and end apart: 2, of which 0 were waited for; matrix products, arithmetic and copies ran while one was open for 9% of the time, Pallas kernels for 24%

profile of v3, /device:TPU:0, one launch (start us, length us, event | category | flops | bytes accessed | tf_op | source)
XLA Modules:
  0.0 84.4 jit_solution(16802797296796151800)
XLA Ops:
  0.0 0.8 broadcast_compare_fusion
  0.8 1.4 %copy.25 = bf16[1024,296]{1,0:T(8,128)(2,1)S(1)} copy(bf16[1024,296]{0,1:T(8,128)(2,1)} %param.13) | data formatting | bytes 1212416 | tf_op args[0]
  2.2 0.2 broadcast_select_fusion.own_ref
  2.5 1.0 %fusion = (bf16[512,296]{1,0:T(8,128)(2,1)}, bf16[512,296]{1,0:T(8,128)(2,1)}) fusion(bf16[1024,296]{1,0:T(8,128)(2,1)S(1)} %broadcast_select_fusion.own_ref), kind=kLoop, calls=%fused_computation.16 | loop fusion | bytes 1212416 | tf_op jit(solution)/shard_map/slice | solution.py:283
  3.5 3.1 %collective-permute-start = (bf16[512,296]{1,0:T(8,128)(2,1)}, bf16[512,296]{1,0:T(8,128)(2,1)}, u32[]{:S(2)}, u32[]{:S(2)}) collective-permute-start(bf16[512,296]{1,0:T(8,128)(2,1)} %get-tuple-element.5), channel_id=1, source_target_pairs={{0,1},{1,2},{2,3},{3,4},{4,5},{5,6},{6,7},{7,8},{8,9},{9,10},{10,1... | collective-permute-start | bytes 909320 | tf_op jit(solution)/shard_map/ppermute | solution.py:18
  6.6 1.3 %collective-permute-start.1 = (bf16[512,296]{1,0:T(8,128)(2,1)}, bf16[512,296]{1,0:T(8,128)(2,1)}, u32[]{:S(2)}, u32[]{:S(2)}) collective-permute-start(bf16[512,296]{1,0:T(8,128)(2,1)} %get-tuple-element.6), channel_id=1, source_target_pairs={{1,0},{2,1},{3,2},{4,3},{5,4},{6,5},{7,6},{8,7},{9,8},{10,9},{11,1... | collective-permute-start | bytes 909320 | tf_op jit(solution)/shard_map/ppermute | solution.py:18
  7.9 0.6 reshape.15
  8.7 0.5 convolution_convert_fusion
  9.3 0.1 reshape.16
  9.5 1.1 %convolution_convert_fusion.3.block_ref = bf16[16,296]{1,0:T(8,128)(2,1)} fusion(bf16[16,2368]{1,0:T(8,128)(2,1)S(1)} %reshape.16, bf16[2368,296]{0,1:T(8,128)(2,1)S(1)} %copy-done), kind=kOutput, calls=%fused_computation.3 | convolution fusion | flops 22434432 | bytes 1487104 | tf_op jit(solution)/shard_map/dot_general | solution.py:24
  10.6 20.4 %shard_map.127 = bf16[8,4,16,296]{3,2,1,0:T(8,128)(2,1)} custom-call(bf16[16,296]{1,0:T(8,128)(2,1)} %convolution_convert_fusion.3.block_ref), custom_call_target="tpu_custom_call" | custom-call | tf_op jit(solution)/shard_map/pallas_call | solution.py:135
  31.0 1.4 %reshape_reshape.3 = bf16[64,2368]{1,0:T(8,128)(2,1)S(1)} reshape(bf16[8,4,16,296]{3,2,1,0:T(8,128)(2,1)} %shard_map.127) | data formatting | bytes 606208 | tf_op jit(solution)/shard_map/reshape;reshape | solution.py:23
  32.4 1.2 %copy.27 = bf16[512,296]{0,1:T(8,128)(2,1)S(1)} copy(bf16[512,296]{1,0:T(8,128)(2,1)} %bitcast.24) | data formatting | bytes 606208 | tf_op jit(solution)/shard_map/reshape | solution.py:149
  33.5 0.6 convolution_convert_fusion.2
  34.1 0.1 copy.28
  34.4 0.6 pad_bitcast_fusion.1
  35.0 0.6 subtract_bitcast_fusion.index_ref
  35.7 1.2 %pad_maximum_fusion = bf16[1024,296]{1,0:T(8,128)(2,1)S(1)} fusion(bf16[512,296]{1,0:T(8,128)(2,1)} %collective-permute-done.1.above_ref, bf16[512,296]{1,0:T(8,128)(2,1)} %collective-permute-done.below_ref), kind=kLoop, calls=%fused_computation.4 | loop fusion | flops 1212416 | bytes 1212416 | tf_op jit(solution)/shard_map/concatenate | solution.py:294
  36.9 0.6 reshape.14
  37.5 0.5 convolution_convert_fusion.1
  38.1 1.4 %concatenate.13 = bf16[832,296]{0,1:T(8,128)(2,1)S(1)} concatenate(bf16[64,296]{0,1:T(8,128)(2,1)S(1)} %get-tuple-element.8, bf16[128,296]{0,1:T(8,128)(2,1)S(1)} %convolution_convert_fusion, bf16[64,296]{0,1:T(8,128)(2,1)S(1)} %get-tuple-element.7, bf16[512,296]{0,1:T(8,128)(2,1)S(1)} %copy.27, bf16[64,296]{0,1:T(8,128)(2,1)S(1)} %copy.28), dimensions={0} | concatenate | bytes 985088 | tf_op jit(solution)/shard_map/concatenate | solution.py:297
  39.5 0.8 %pad_bitcast_fusion.table_ref = bf16[296,896]{1,0:T(8,128)(2,1)} fusion(bf16[832,296]{0,1:T(8,128)(2,1)S(1)} %concatenate.13), kind=kLoop, calls=%fused_computation.6 | loop fusion | bytes 1022976 | tf_op jit(solution)/shard_map/transpose | solution.py:318
  40.4 29.1 %shard_map.128.near_ref = f32[296,1024]{1,0:T(8,128)} custom-call(bf16[512,296]{1,0:T(8,128)(2,1)} %collective-permute-done.below_ref, bf16[1024,296]{1,0:T(8,128)(2,1)} %copy-done.1, bf16[512,296]{1,0:T(8,128)(2,1)} %collective-permute-done.1.above_ref, s32[8,1024]{1,0:T(8,128)} %subtract_bitcast_fusion.index_ref, s32[8,1024]{1,0:T(8,128)} %bitcast.25, ...), custom_call_target="tpu_custom_call" | custom-call | flops 13191086080 | bytes 5607424 | tf_op jit(solution)/shard_map/pallas_call | solution.py:181
  69.5 14.8 %shard_map.129 = bf16[296,1024]{1,0:T(8,128)(2,1)} custom-call(bf16[296,896]{1,0:T(8,128)(2,1)} %pad_bitcast_fusion.table_ref, s32[8,256]{1,0:T(8,128)} %get-tuple-element.10.index_ref, s32[8,256]{1,0:T(8,128)} %get-tuple-element.9.class_ref, bf16[296,9472]{1,0:T(8,128)(2,1)} %bitcast.23, bf16[296,2368]{1,0:T(8,128)(2,1)} %down_ref.1, ...), custom_call_target="tpu_custom_call" | custom-call | flops 1435500544 | bytes 5607424 | tf_op jit(solution)/shard_map/pallas_call | solution.py:237
  (29 shorter events, 0.6 us)
Async XLA Ops:
  0.0 8.7 %copy-start = (bf16[2368,296]{0,1:T(8,128)(2,1)S(1)}, bf16[2368,296]{0,1:T(8,128)(2,1)}, u32[]{:S(2)}) copy-start(bf16[2368,296]{0,1:T(8,128)(2,1)} %param.15) | copy-start | bytes 4205572
  2.5 6.0 %copy-start.1 = (bf16[1024,296]{1,0:T(8,128)(2,1)}, bf16[1024,296]{1,0:T(8,128)(2,1)S(1)}, u32[]{:S(2)}) copy-start(bf16[1024,296]{1,0:T(8,128)(2,1)S(1)} %broadcast_select_fusion.own_ref) | copy-start | bytes 1818628
  2.5 6.0 %copy-start.5 = (s32[16,8]{0,1:T(8,128)S(1)}, s32[16,8]{0,1:T(8,128)}, u32[]{:S(2)}) copy-start(s32[16,8]{0,1:T(8,128)} %param.22) | copy-start | bytes 1540
  2.5 6.0 %copy-start.7 = (s32[2,8]{1,0:T(2,128)S(1)}, s32[2,8]{1,0:T(2,128)}, u32[]{:S(2)}) copy-start(s32[2,8]{1,0:T(2,128)} %param.24) | copy-start | bytes 196
  2.5 6.1 %copy-start.8 = (s32[2,8]{1,0:T(2,128)S(1)}, s32[2,8]{1,0:T(2,128)}, u32[]{:S(2)}) copy-start(s32[2,8]{1,0:T(2,128)} %param.25) | copy-start | bytes 196
  3.5 32.2 %collective-permute-start = (bf16[512,296]{1,0:T(8,128)(2,1)}, bf16[512,296]{1,0:T(8,128)(2,1)}, u32[]{:S(2)}, u32[]{:S(2)}) collective-permute-start(bf16[512,296]{1,0:T(8,128)(2,1)} %get-tuple-element.5), channel_id=1, source_target_pairs={{0,1},{1,2},{2,3},{3,4},{4,5},{5,6},{6,7},{7,8},{8,9},{9,10},{10,1... | collective-permute-start | bytes 909320 | tf_op jit(solution)/shard_map/ppermute | solution.py:18
  6.6 29.1 %collective-permute-start.1 = (bf16[512,296]{1,0:T(8,128)(2,1)}, bf16[512,296]{1,0:T(8,128)(2,1)}, u32[]{:S(2)}, u32[]{:S(2)}) collective-permute-start(bf16[512,296]{1,0:T(8,128)(2,1)} %get-tuple-element.6), channel_id=1, source_target_pairs={{1,0},{2,1},{3,2},{4,3},{5,4},{6,5},{7,6},{8,7},{9,8},{10,9},{11,1... | collective-permute-start | bytes 909320 | tf_op jit(solution)/shard_map/ppermute | solution.py:18
  32.3 1.9 %copy-start.6 = (s32[128,8]{0,1:T(8,128)S(1)}, s32[128,8]{0,1:T(8,128)}, u32[]{:S(2)}) copy-start(s32[128,8]{0,1:T(8,128)} %param.20) | copy-start | bytes 12292
  32.3 2.0 %copy-start.3 = (s32[16,8]{0,1:T(8,128)S(1)}, s32[16,8]{0,1:T(8,128)}, u32[]{:S(2)}) copy-start(s32[16,8]{0,1:T(8,128)} %param.23) | copy-start | bytes 1540
  32.3 2.0 %copy-start.4 = (s32[128,8]{0,1:T(8,128)S(1)}, s32[128,8]{0,1:T(8,128)}, u32[]{:S(2)}) copy-start(s32[128,8]{0,1:T(8,128)} %param.21) | copy-start | bytes 12292
  32.4 2.7 %copy-start.2 = (s32[1024,8]{0,1:T(8,128)S(1)}, s32[1024,8]{0,1:T(8,128)}, u32[]{:S(2)}) copy-start(s32[1024,8]{0,1:T(8,128)} %param.18) | copy-start | bytes 98308
